TPU v7x, 32 devices: a whole 2x2x4 slice. The times are simulated.
32 devices in a mesh: group: 4 (over y, core), dev: 8 (over z, x).
Axes of the slice: x: 2, y: 2, z: 4, core: 2. Of those that a mesh axis runs over, the one named last changes fastest.
Arguments:
- node_state: bfloat16 [16384, 512], P(('group', 'dev')), may hold values from -6 to 6
- hub_state: bfloat16 [64, 512], P('dev'), may hold values from -6 to 6
- w_edge_in: bfloat16 [512, 256], replicated, may hold values from -0.25 to 0.25
- w_edge_out: bfloat16 [256, 512], replicated, may hold values from -0.375 to 0.375
- w_update: bfloat16 [512, 512], replicated, may hold values from -0.25 to 0.25
- edge_src: int32 [131072], P(('group', 'dev')), may hold values from 0 to 319
- edge_dst: int32 [131072], P(('group', 'dev')), may hold values from 0 to 319
- edge_mask: int32 [131072], P(('group', 'dev')), may hold values 0 or 1
- send_list: int32 [32, 8, 32], P(('group', 'dev')), may hold values from 0 to 511
- send_count: int32 [32, 8], P(('group', 'dev')), may hold values from 8 to 32, as said below
- node_cot: bfloat16 [16384, 512], P(('group', 'dev')), may hold values from -0.059814453 to 0.059814453
- hub_cot: bfloat16 [64, 512], P('dev'), may hold values from -0.059814453 to 0.059814453
Outputs:
- new_state: bfloat16 [16384, 512], P(('group', 'dev'))
- new_hub: bfloat16 [64, 512], P('dev')
- grad_in: float32 [512, 256], replicated
- grad_out: float32 [256, 512], replicated
- grad_update: float32 [512, 512], replicated
Inputs may be any that keep to these rules, and one draw needn't show every extreme that they name: Device 0 sends 32 live slots to peer 0: send_count[0, 0] = 32.
All inputs are finite; a program needn't handle non-finite values. No bound on the sum of `edge_mask` on one device may be relied on, other than what follows from the above.
Results may differ from a plain program's by a relative error of at most 0.0064.
The roundings to bfloat16 on the way count: a program that leaves them out, or rounds other values in their place, can miss the bound.
Values may be sent and summed in bfloat16 or wider, within the bound.
No kernel may reach another device: no remote copies, remote signals or barrier semaphores. Data moves between devices by JAX's collectives and lax.ppermute only.
A program may use at most 64 MiB of HBM per device.

v0:
```python
import jax
import jax.numpy as jnp
from jax import lax
from jax.sharding import PartitionSpec as P


def silu_grad(values):
    sigmoid_v = jax.nn.sigmoid(values)
    return sigmoid_v * (1.0 + values * (1.0 - sigmoid_v))


def finish(states, summed, degree, w_update):
    mean_part = summed / jnp.maximum(degree, 1.0)[:, None]
    mixed_rows = (states.astype(jnp.float32) + mean_part).astype(jnp.bfloat16)
    pre_update = jnp.dot(mixed_rows, w_update, preferred_element_type=jnp.float32)
    updated = (states.astype(jnp.float32) + jax.nn.silu(pre_update)).astype(jnp.bfloat16)
    return (mixed_rows, pre_update, updated)


def backward_rows(cotangent, pre_update, degree, w_update):
    grad_pre = (cotangent.astype(jnp.float32) * silu_grad(pre_update)).astype(jnp.bfloat16)
    grad_mix = jnp.dot(grad_pre, w_update.T, preferred_element_type=jnp.float32)
    grad_sum = (grad_mix / jnp.maximum(degree, 1.0)[:, None]).astype(jnp.bfloat16)
    return (grad_pre, grad_sum)


def shards(
    node_state,
    hub_state,
    w_edge_in,
    w_edge_out,
    w_update,
    edge_src,
    edge_dst,
    edge_mask,
    send_list,
    send_count,
    node_cot,
    hub_cot,
):
    width = node_state.shape[1]
    master_rows = node_state.shape[0]
    send_rows = send_list[0]
    peer_total = send_rows.shape[0]
    slot_width = send_rows.shape[1]
    mirror_total = peer_total * slot_width
    live_slot = jnp.arange(slot_width)[None, :] < send_count[0][:, None]
    flat_rows = send_rows.reshape(-1)
    flat_live = live_slot.reshape(-1)
    selector = (
        (flat_rows[:, None] == jnp.arange(master_rows)[None, :]) & flat_live[:, None]
    ).astype(jnp.bfloat16)
    contract = (((0,), (0,)), ((), ()))
    outgoing = jnp.dot(selector, node_state, preferred_element_type=jnp.float32).astype(
        jnp.bfloat16
    )
    mirror_rows = lax.all_to_all(
        outgoing.reshape(peer_total, slot_width, width),
        "dev",
        split_axis=0,
        concat_axis=0,
        tiled=True,
    )
    hub_table = lax.all_gather(hub_state, "dev", axis=0, tiled=True)
    local_table = jnp.concatenate([mirror_rows.reshape(mirror_total, width), hub_table], axis=0)
    local_rows = local_table.shape[0]
    edge_total = edge_src.shape[0]
    block_size = min(1024, edge_total)
    block_count = edge_total // block_size
    sources = edge_src.reshape(block_count, block_size)
    targets = edge_dst.reshape(block_count, block_size)
    edge_keep = edge_mask.reshape(block_count, block_size)
    row_ids = jnp.arange(local_rows)[None, :]

    def forward_step(totals, pieces):
        source_ids, target_ids, keep_ids = pieces
        gathered = local_table[source_ids]
        pre_act = jnp.dot(gathered, w_edge_in, preferred_element_type=jnp.float32)
        hidden = jax.nn.silu(pre_act).astype(jnp.bfloat16)
        message = jnp.dot(hidden, w_edge_out, preferred_element_type=jnp.float32).astype(
            jnp.bfloat16
        )
        onehot = ((target_ids[:, None] == row_ids) & (keep_ids[:, None] > 0)).astype(jnp.bfloat16)
        added = lax.dot_general(onehot, message, contract, preferred_element_type=jnp.float32)
        tally = jnp.sum(onehot, axis=0, dtype=jnp.float32)
        return ((totals[0] + added, totals[1] + tally), pre_act)

    start_fwd = (jnp.zeros((local_rows, width), jnp.float32), jnp.zeros((local_rows,), jnp.float32))
    (partial_value, counts_local), saved_acts = lax.scan(
        forward_step, start_fwd, (sources, targets, edge_keep)
    )
    mirror_part = (
        partial_value[:mirror_total].reshape(peer_total, slot_width, width).astype(jnp.bfloat16)
    )
    mirror_count = counts_local[:mirror_total].reshape(peer_total, slot_width).astype(jnp.bfloat16)
    back_part, back_count = (
        lax.all_to_all(mirror_part, "dev", split_axis=0, concat_axis=0, tiled=True),
        lax.all_to_all(mirror_count, "dev", split_axis=0, concat_axis=0, tiled=True),
    )
    summed = lax.dot_general(
        selector,
        back_part.reshape(mirror_total, width),
        contract,
        preferred_element_type=jnp.float32,
    )
    degree = lax.dot_general(
        selector, back_count.reshape(mirror_total, 1), contract, preferred_element_type=jnp.float32
    )[:, 0]
    hub_part = partial_value[mirror_total:]
    hub_count = counts_local[mirror_total:]
    whole_part, whole_count = (
        lax.psum(hub_part.astype(jnp.bfloat16), "group").astype(jnp.float32),
        lax.psum(hub_count.astype(jnp.bfloat16), "group").astype(jnp.float32),
    )
    hub_summed, hub_degree = (
        lax.psum_scatter(
            whole_part.astype(jnp.bfloat16), "dev", scatter_dimension=0, tiled=True
        ).astype(jnp.float32),
        lax.psum_scatter(
            whole_count.astype(jnp.bfloat16), "dev", scatter_dimension=0, tiled=True
        ).astype(jnp.float32),
    )
    mixed_rows, pre_update, new_state = finish(node_state, summed, degree, w_update)
    hub_mixed, hub_pre, new_hub = finish(hub_state, hub_summed, hub_degree, w_update)
    grad_pre, grad_sum = backward_rows(node_cot, pre_update, degree, w_update)
    hub_grad_pre, hub_grad_sum = backward_rows(hub_cot, hub_pre, hub_degree, w_update)
    grad_outgoing = jnp.dot(selector, grad_sum, preferred_element_type=jnp.float32).astype(
        jnp.bfloat16
    )
    grad_mirror = lax.all_to_all(
        grad_outgoing.reshape(peer_total, slot_width, width),
        "dev",
        split_axis=0,
        concat_axis=0,
        tiled=True,
    )
    grad_hubs = lax.all_gather(hub_grad_sum, "dev", axis=0, tiled=True)
    grad_table = jnp.concatenate([grad_mirror.reshape(mirror_total, width), grad_hubs], axis=0)
    hub_weight = (lax.axis_index("group") == 0).astype(jnp.float32)
    grad_update = lax.dot_general(
        mixed_rows, grad_pre, contract, preferred_element_type=jnp.float32
    )
    grad_update = grad_update + hub_weight * lax.dot_general(
        hub_mixed, hub_grad_pre, contract, preferred_element_type=jnp.float32
    )

    def backward_step(totals, pieces):
        source_ids, target_ids, keep_ids, pre_act = pieces
        gathered = local_table[source_ids]
        hidden = jax.nn.silu(pre_act).astype(jnp.bfloat16)
        grad_message = jnp.where(
            keep_ids[:, None] > 0, grad_table[target_ids], jnp.zeros((), jnp.bfloat16)
        )
        grad_w_out = lax.dot_general(
            hidden, grad_message, contract, preferred_element_type=jnp.float32
        )
        grad_hidden = jnp.dot(grad_message, w_edge_out.T, preferred_element_type=jnp.float32)
        grad_act = (grad_hidden * silu_grad(pre_act)).astype(jnp.bfloat16)
        grad_w_in = lax.dot_general(
            gathered, grad_act, contract, preferred_element_type=jnp.float32
        )
        return ((totals[0] + grad_w_in, totals[1] + grad_w_out), None)

    start = (jnp.zeros(w_edge_in.shape, jnp.float32), jnp.zeros(w_edge_out.shape, jnp.float32))
    local_grads, _ = lax.scan(backward_step, start, (sources, targets, edge_keep, saved_acts))
    grad_in, grad_out, grad_upd = lax.psum(
        (local_grads[0], local_grads[1], grad_update), ("group", "dev")
    )
    return (new_state, new_hub, grad_in, grad_out, grad_upd)


def solution(mesh):
    return jax.shard_map(
        shards,
        mesh=mesh,
        in_specs=(
            P(("group", "dev"), None),
            P("dev", None),
            P(),
            P(),
            P(),
            P(("group", "dev")),
            P(("group", "dev")),
            P(("group", "dev")),
            P(("group", "dev"), None, None),
            P(("group", "dev"), None),
            P(("group", "dev"), None),
            P("dev", None),
        ),
        out_specs=(P(("group", "dev"), None), P("dev", None), P(), P(), P()),
        check_vma=False,
    )
```

profile of v0, /device:TPU:0, one launch (start us, length us, event | category | flops | bytes accessed | tf_op | source)
XLA Modules:
  0.0 417.0 jit_solution(8544541724577750692)
XLA Ops:
  8.8 2.1 convolution_convert_fusion.1
  10.9 7.2 %all-to-all-start = ((bf16[8,32,512]{2,1,0:T(8,128)(2,1)}), bf16[8,32,512]{2,1,0:T(8,128)(2,1)S(1)}, u32[]{:S(2)}, u32[]{:S(2)}) async-start(bf16[8,32,512]{2,1,0:T(8,128)(2,1)} %bitcast.1), calls=%async_computation | async-start | bytes 524288 | tf_op jit(solution)/shard_map/all_to_all | solution.py:57
  20.4 31.2 %all_gather.6 = bf16[64,512]{1,0:T(8,128)(2,1)S(1)} all-gather(bf16[8,512]{1,0:T(8,128)(2,1)} %param.17), channel_id=1, replica_groups=mesh['group'=4,'dev'=8] {'dev'}, dimensions={0}, use_global_device_ids=true | all-gather | bytes 73728 | tf_op jit(solution)/shard_map/all_gather | solution.py:64
  51.7 33.4 %while.28 = (s32[]{:T(128)}, f32[320,512]{1,0:T(8,128)}, f32[320]{0:T(512)S(1)}, f32[4,1024,256]{2,1,0:T(8,128)}, s32[4,1024]{1,0:T(4,128)S(1)}, /*index=5*/s32[...) while((s32[]{:T(128)}, f32[320,512]{1,0:T(8,128)}, ...), condition=%wide.region_2.3_spmd.clone, body=%wide.region_0.2_spmd.clone.sunk | while | flops 876877120 | bytes 10273476 | solution.py:89
  51.8 4.0 gather_fusion
  55.7 1.4 bitcast_dynamic-update-slice_fusion.2
  57.2 1.7 fusion.93
  59.3 4.0 gather_fusion
  63.3 1.5 bitcast_dynamic-update-slice_fusion.2
  64.8 2.7 fusion.93
  67.9 4.0 gather_fusion
  71.9 1.4 bitcast_dynamic-update-slice_fusion.2
  73.4 2.7 fusion.93
  76.5 4.0 gather_fusion
  80.5 1.4 bitcast_dynamic-update-slice_fusion.2
  82.0 2.7 fusion.93
  85.8 5.4 %all-to-all-start.2 = ((bf16[8,1,32]{2,1,0:T(2,128)(2,1)}), bf16[8,1,32]{2,1,0:T(2,128)(2,1)S(1)}, u32[]{:S(2)}, u32[]{:S(2)}) async-start(bf16[8,1,32]{2,1,0:T(2,128)(2,1)} %convert_element_type.118), calls=%async_computation.2 | async-start | bytes 8192 | tf_op jit(solution)/shard_map/all_to_all | solution.py:98
  95.1 21.8 %all-reduce = bf16[64]{0:T(256)(128)(2,1)S(1)} all-reduce(bf16[64]{0:T(256)(128)(2,1)S(1)} %slice.27), channel_id=3, replica_groups=mesh['group'=4,'dev'=8] {'dev'}, use_global_device_ids=true, to_apply=%region_6.7.clone | all-reduce | flops 64 | bytes 256
  117.0 3.4 all-to-all-start.1
  120.8 38.2 %reduce-scatter.2.cloned.1.call-done = bf16[8,512]{1,0:T(8,128)(2,1)} async-done(((bf16[64,512]{1,0:T(8,128)(2,1)}), bf16[8,512]{1,0:T(8,128)(2,1)}) %reduce-scatter.2.cloned.1.call-update) | async-done | bytes 8208 | tf_op jit(solution)/shard_map/reduce_scatter | solution.py:116
  159.0 6.0 %all-reduce.2 = (bf16[8,512]{1,0:T(8,128)(2,1)S(1)}, bf16[8]{0:T(256)(128)(2,1)S(1)}) all-reduce(bf16[8,512]{1,0:T(8,128)(2,1)} %reduce-scatter.2.cloned.1.call-done, bf16[8]{0:T(256)(128)(2,1)S(1)} %dynamic-slice.1), channel_id=1, replica_groups=mesh['group'=4,'dev'=8] {'group'}, use_global_device_ids=true, to_apply=%region_3.4 | all-reduce | flops 4104 | bytes 16416 | tf_op jit(solution)/shard_map/psum | solution.py:112
  166.1 30.5 %all_gather.7 = bf16[64,512]{1,0:T(8,128)(2,1)S(1)} all-gather(bf16[8,512]{1,0:T(8,128)(2,1)S(1)} %fusion.42), channel_id=1, replica_groups=mesh['group'=4,'dev'=8] {'dev'}, dimensions={0}, use_global_device_ids=true | all-gather | bytes 73728 | tf_op jit(solution)/shard_map/all_gather | solution.py:137
  196.6 1.5 fusion.38
  198.2 2.7 multiply_convert_fusion.3
  200.9 1.4 fusion.41
  202.3 3.6 all-to-all-start.3
  207.8 6.3 %all-to-all-done.3 = bf16[8,32,512]{2,1,0:T(8,128)(2,1)S(1)} async-done(((bf16[8,32,512]{2,1,0:T(8,128)(2,1)}), bf16[8,32,512]{2,1,0:T(8,128)(2,1)S(1)}, u32[]{:S(2)}, u32[]{:S(2)}) %all-to-all-start.3) | async-done | bytes 262176 | tf_op jit(solution)/shard_map/all_to_all | solution.py:130
  214.1 56.7 %while.29 = (s32[]{:T(128)}, f32[512,256]{1,0:T(8,128)}, f32[256,512]{1,0:T(8,128)}, s32[4,1024]{1,0:T(4,128)S(1)}, bf16[320,512]{1,0:T(8,128)(2,1)S(1)}, /*inde...) while((s32[]{:T(128)}, f32[512,256]{1,0:T(8,128)}, ...), condition=%wide.region_8.9_spmd.clone, body=%wide.region_7.8_spmd.clone.sunk | while | flops 810558464 | bytes 11845768 | solution.py:165
  214.2 4.0 gather_fusion.2
  218.2 4.0 gather_fusion.1
  222.2 3.3 convolution_add_fusion.4
  225.5 2.6 convolution_add_fusion.5
  228.1 4.0 gather_fusion.2
  232.1 4.0 gather_fusion.1
  236.1 3.4 convolution_add_fusion.4
  239.6 2.8 convolution_add_fusion.5
  242.4 4.0 gather_fusion.2
  246.3 4.0 gather_fusion.1
  250.4 3.4 convolution_add_fusion.4
  253.8 2.8 convolution_add_fusion.5
  256.6 4.0 gather_fusion.2
  260.6 4.0 gather_fusion.1
  264.6 3.4 convolution_add_fusion.4
  268.0 2.7 convolution_add_fusion.5
  270.8 133.3 %all-reduce.5.cloned.1.call-done = (f32[512,256]{1,0:T(8,128)}, f32[256,512]{1,0:T(8,128)}, f32[512,512]{1,0:T(8,128)}) async-done(((f32[512,256]{1,0:T(8,128)}, f32[256,512]{1,0:T(8,128)}, f32[512,512]{1,0:T(8,128)}), (f32[512,256]{1,0:T(8,128)}, f32[256,512]{1,0:T(8,128)}, f32[512,512]{1,0:T(8,128)})) %all-reduce.5.cloned.1.call-update) | async-done | bytes 2097168 | tf_op jit(solution)/shard_map/psum | solution.py:166
  404.1 1.9 copy.44
  406.0 1.9 copy.45
  407.9 2.3 copy.46
  (104 shorter events, 13.1 us)
Async XLA Ops:
  7.2 157.8 %copy-start = (bf16[512,512]{1,0:T(8,128)(2,1)S(1)}, bf16[512,512]{1,0:T(8,128)(2,1)}, u32[]{:S(2)}) copy-start(bf16[512,512]{1,0:T(8,128)(2,1)} %param.20) | copy-start | bytes 1572868
  10.9 40.7 %all-to-all-start = ((bf16[8,32,512]{2,1,0:T(8,128)(2,1)}), bf16[8,32,512]{2,1,0:T(8,128)(2,1)S(1)}, u32[]{:S(2)}, u32[]{:S(2)}) async-start(bf16[8,32,512]{2,1,0:T(8,128)(2,1)} %bitcast.1), calls=%async_computation | async-start | bytes 524288 | tf_op jit(solution)/shard_map/all_to_all | solution.py:57
  51.7 39.6 %copy-start.6 = (u32[32]{0:T(128)S(1)}, u32[32]{0:T(128)}, u32[]{:S(2)}) copy-start(u32[32]{0:T(128)} %constant.65) | copy-start | bytes 388
  51.7 113.3 %copy-start.2 = (bf16[8,512]{1,0:T(8,128)(2,1)S(1)}, bf16[8,512]{1,0:T(8,128)(2,1)}, u32[]{:S(2)}) copy-start(bf16[8,512]{1,0:T(8,128)(2,1)} %param.17) | copy-start | bytes 24580
  51.7 114.2 %copy-start.3 = (bf16[8,512]{1,0:T(8,128)(2,1)S(1)}, bf16[8,512]{1,0:T(8,128)(2,1)}, u32[]{:S(2)}) copy-start(bf16[8,512]{1,0:T(8,128)(2,1)} %param.27) | copy-start | bytes 24580
  51.7 4.0 copy-start.1
  51.8 5.5 %copy-start.5 = (bf16[256,512]{1,0:T(8,128)(2,1)S(1)}, bf16[256,512]{1,0:T(8,128)(2,1)}, u32[]{:S(2)}) copy-start(bf16[256,512]{1,0:T(8,128)(2,1)} %get-tuple-element.406) | copy-start | bytes 786436 | tf_op jit(solution)/shard_map/while
  59.2 4.0 copy-start.1
  59.3 5.5 %copy-start.5 = (bf16[256,512]{1,0:T(8,128)(2,1)S(1)}, bf16[256,512]{1,0:T(8,128)(2,1)}, u32[]{:S(2)}) copy-start(bf16[256,512]{1,0:T(8,128)(2,1)} %get-tuple-element.406) | copy-start | bytes 786436 | tf_op jit(solution)/shard_map/while
  67.9 4.0 copy-start.1
  67.9 5.5 %copy-start.5 = (bf16[256,512]{1,0:T(8,128)(2,1)S(1)}, bf16[256,512]{1,0:T(8,128)(2,1)}, u32[]{:S(2)}) copy-start(bf16[256,512]{1,0:T(8,128)(2,1)} %get-tuple-element.406) | copy-start | bytes 786436 | tf_op jit(solution)/shard_map/while
  76.5 4.0 copy-start.1
  76.5 5.5 %copy-start.5 = (bf16[256,512]{1,0:T(8,128)(2,1)S(1)}, bf16[256,512]{1,0:T(8,128)(2,1)}, u32[]{:S(2)}) copy-start(bf16[256,512]{1,0:T(8,128)(2,1)} %get-tuple-element.406) | copy-start | bytes 786436 | tf_op jit(solution)/shard_map/while
  85.8 31.2 %all-to-all-start.2 = ((bf16[8,1,32]{2,1,0:T(2,128)(2,1)}), bf16[8,1,32]{2,1,0:T(2,128)(2,1)S(1)}, u32[]{:S(2)}, u32[]{:S(2)}) async-start(bf16[8,1,32]{2,1,0:T(2,128)(2,1)} %convert_element_type.118), calls=%async_computation.2 | async-start | bytes 8192 | tf_op jit(solution)/shard_map/all_to_all | solution.py:98
  91.2 67.8 %reduce-scatter.2.cloned.1.call-start = ((), (), s32[]{:S(2)}) async-start(), calls=%async_computation.5 | async-start | bytes 73728 | tf_op jit(solution)/shard_map/reduce_scatter | solution.py:116
  92.5 105.6 %copy-start.4 = (bf16[512,512]{1,0:T(8,128)(2,1)S(1)}, bf16[512,512]{1,0:T(8,128)(2,1)}, u32[]{:S(2)}) copy-start(bf16[512,512]{1,0:T(8,128)(2,1)} %param.26) | copy-start | bytes 1572868
  117.0 79.6 %all-to-all-start.1 = ((bf16[8,32,512]{2,1,0:T(8,128)(2,1)}), bf16[8,32,512]{2,1,0:T(8,128)(2,1)S(1)}, u32[]{:S(2)}, u32[]{:S(2)}) async-start(bf16[8,32,512]{2,1,0:T(8,128)(2,1)} %bitcast.3), calls=%async_computation.1 | async-start | bytes 524288 | tf_op jit(solution)/shard_map/all_to_all | solution.py:97
  202.3 11.8 %all-to-all-start.3 = ((bf16[8,32,512]{2,1,0:T(8,128)(2,1)}), bf16[8,32,512]{2,1,0:T(8,128)(2,1)S(1)}, u32[]{:S(2)}, u32[]{:S(2)}) async-start(bf16[8,32,512]{2,1,0:T(8,128)(2,1)} %bitcast.6), calls=%async_computation.3 | async-start | bytes 524288 | tf_op jit(solution)/shard_map/all_to_all | solution.py:130
  205.9 198.3 %all-reduce.5.cloned.1.call-start = ((), (), s32[]{:S(2)}) async-start(), calls=%async_computation.6 | async-start | bytes 4194304 | tf_op jit(solution)/shard_map/psum | solution.py:166
Sparse Core Ops, SparseCore 0:
  96.0 62.9 reduce-scatter.1
  270.9 133.1 all-reduce.4
where the time goes:
time: 418 us; the launch traced here: 417 us
  waiting for transfers between devices  178 us (43%)
  blocking collectives  89.5 us (21%)
  local copies, waits for them, and re-layouts  59.5 us (14%)
  matrix products  51.1 us (12%)
  starting transfers between devices  19.8 us (5%)
  between operations  14.9 us (4%)
    psum x1, waiting for transfers between devices, shards(): lax.psum((local_grads[0], local_grads[1], grad_update), ('group', 'dev'))  133 us
    reduce_scatter x1, waiting for transfers between devices, shards(): lax.psum_scatter(whole_part.astype(jnp.bfloat16), 'dev', scatter_dimensio...  38.2 us
    all_gather x1, blocking collectives, shards(): hub_table = lax.all_gather(hub_state, 'dev', axis=0, tiled=True)  31.2 us
    all_gather x1, blocking collectives, shards(): grad_hubs = lax.all_gather(hub_grad_sum, 'dev', axis=0, tiled=True)  30.5 us
    unnamed x1, blocking collectives  21.8 us
    gather x4, local copies, waits for them, and re-layouts, backward_step(): grad_table[target_ids]  15.9 us
    gather x4, local copies, waits for them, and re-layouts, backward_step(): gathered = local_table[source_ids]  15.9 us
    gather x4, local copies, waits for them, and re-layouts, forward_step(): gathered = local_table[source_ids]  15.9 us
  transfers between devices with their start and end apart: 6, of which 3 were waited for; matrix products, arithmetic and copies ran while one was open for 2% of the time, Pallas kernels for 0%

commit v1 on v0

--- a/solution.py
+++ b/solution.py
@@ -127,13 +127,16 @@
     grad_outgoing = jnp.dot(selector, grad_sum, preferred_element_type=jnp.float32).astype(
         jnp.bfloat16
     )
-    grad_mirror = lax.all_to_all(
-        grad_outgoing.reshape(peer_total, slot_width, width),
-        "dev",
-        split_axis=0,
-        concat_axis=0,
-        tiled=True,
-    )
+    x = grad_outgoing.reshape(peer_total, slot_width, width)
+    ways, here = (lax.axis_size("dev"), lax.axis_index("dev"))
+    width_2 = x.shape[0] // ways
+    turned = jnp.roll(x, -here * width_2, axis=0)
+    got = [lax.slice_in_dim(turned, 0, width_2, axis=0)]
+    for far in range(1, ways):
+        sent = lax.slice_in_dim(turned, far * width_2, (far + 1) * width_2, axis=0)
+        got.append(lax.ppermute(sent, "dev", [(d, (d + far) % ways) for d in range(ways)]))
+    line = jnp.concatenate(got[::-1], axis=0)
+    grad_mirror = jnp.roll(line, (here + 1) * got[0].shape[0], axis=0)
     grad_hubs = lax.all_gather(hub_grad_sum, "dev", axis=0, tiled=True)
     grad_table = jnp.concatenate([grad_mirror.reshape(mirror_total, width), grad_hubs], axis=0)
     hub_weight = (lax.axis_index("group") == 0).astype(jnp.float32)

time: 418 us -> 422 us (level)
  starting transfers between devices: 19.8 us -> 25 us
    ppermute x0 -> x7, starting transfers between devices: none -> 8.8 us  [shards(): lax.ppermute(sent, 'dev', [(d, (d + far) % ways) for d in range(ways)])]
    all_to_all x1 -> x0, waiting for transfers between devices: 6.32 us -> none  [shards(): lax.all_to_all(grad_outgoing.reshape(peer_total, slot_width, width), 'dev...]
    ppermute x0 -> x7, waiting for transfers between devices: none -> 5.11 us  [shards(): lax.ppermute(sent, 'dev', [(d, (d + far) % ways) for d in range(ways)])]
  transfers between devices with their start and end apart: 6 -> 12, of which waited for: 3 -> 5; matrix products, arithmetic and copies ran while one was open for 2% -> 2% of each run, Pallas kernels for 0% -> 0%
where the time goes in v1:
time: 422 us; the launch traced here: 421 us
  waiting for transfers between devices  177 us (42%)
  blocking collectives  89.5 us (21%)
  local copies, waits for them, and re-layouts  59.6 us (14%)
  matrix products  50.4 us (12%)
  starting transfers between devices  25 us (6%)
  between operations  15 us (4%)
    psum x1, waiting for transfers between devices, shards(): lax.psum((local_grads[0], local_grads[1], grad_update), ('group', 'dev'))  134 us
    reduce_scatter x1, waiting for transfers between devices, shards(): lax.psum_scatter(whole_part.astype(jnp.bfloat16), 'dev', scatter_dimensio...  38.2 us
    all_gather x1, blocking collectives, shards(): hub_table = lax.all_gather(hub_state, 'dev', axis=0, tiled=True)  31.2 us
    all_gather x1, blocking collectives, shards(): grad_hubs = lax.all_gather(hub_grad_sum, 'dev', axis=0, tiled=True)  30.5 us
    unnamed x1, blocking collectives  21.8 us
    gather x4, local copies, waits for them, and re-layouts, forward_step(): gathered = local_table[source_ids]  15.9 us
    gather x4, local copies, waits for them, and re-layouts, backward_step(): grad_table[target_ids]  15.9 us
    gather x4, local copies, waits for them, and re-layouts, backward_step(): gathered = local_table[source_ids]  15.9 us
  transfers between devices with their start and end apart: 12, of which 5 were waited for; matrix products, arithmetic and copies ran while one was open for 2% of the time, Pallas kernels for 0%

profile of v1, /device:TPU:0, one launch (start us, length us, event | category | flops | bytes accessed | tf_op | source)
XLA Modules:
  0.0 420.9 jit_solution(12386570361111681003)
XLA Ops:
  8.8 2.1 convolution_convert_fusion.1
  10.9 7.2 %all-to-all-start = ((bf16[8,32,512]{2,1,0:T(8,128)(2,1)}), bf16[8,32,512]{2,1,0:T(8,128)(2,1)S(1)}, u32[]{:S(2)}, u32[]{:S(2)}) async-start(bf16[8,32,512]{2,1,0:T(8,128)(2,1)} %bitcast.1), calls=%async_computation | async-start | bytes 524288 | tf_op jit(solution)/shard_map/all_to_all | solution.py:57
  20.4 31.2 %all_gather.6 = bf16[64,512]{1,0:T(8,128)(2,1)S(1)} all-gather(bf16[8,512]{1,0:T(8,128)(2,1)} %param.19), channel_id=1, replica_groups=mesh['group'=4,'dev'=8] {'dev'}, dimensions={0}, use_global_device_ids=true | all-gather | bytes 73728 | tf_op jit(solution)/shard_map/all_gather | solution.py:64
  51.7 33.3 %while.28 = (s32[]{:T(128)}, f32[320,512]{1,0:T(8,128)}, f32[320]{0:T(512)S(1)}, f32[4,1024,256]{2,1,0:T(8,128)}, s32[4,1024]{1,0:T(4,128)S(1)}, /*index=5*/s32[...) while((s32[]{:T(128)}, f32[320,512]{1,0:T(8,128)}, ...), condition=%wide.region_2.3_spmd.clone, body=%wide.region_0.2_spmd.clone.sunk | while | flops 876877120 | bytes 10273476 | solution.py:89
  51.8 4.0 gather_fusion
  57.2 1.7 fusion.96
  59.3 4.0 gather_fusion
  63.3 1.4 bitcast_dynamic-update-slice_fusion.2
  64.8 2.7 fusion.96
  67.9 4.0 gather_fusion
  73.3 2.7 fusion.96
  76.5 4.0 gather_fusion
  82.0 2.7 fusion.96
  85.7 5.4 %all-to-all-start.2 = ((bf16[8,1,32]{2,1,0:T(2,128)(2,1)}), bf16[8,1,32]{2,1,0:T(2,128)(2,1)S(1)}, u32[]{:S(2)}, u32[]{:S(2)}) async-start(bf16[8,1,32]{2,1,0:T(2,128)(2,1)} %convert_element_type.118), calls=%async_computation.2 | async-start | bytes 8192 | tf_op jit(solution)/shard_map/all_to_all | solution.py:98
  95.1 21.8 %all-reduce = bf16[64]{0:T(256)(128)(2,1)S(1)} all-reduce(bf16[64]{0:T(256)(128)(2,1)S(1)} %slice.51), channel_id=3, replica_groups=mesh['group'=4,'dev'=8] {'dev'}, use_global_device_ids=true, to_apply=%region_6.7.clone | all-reduce | flops 64 | bytes 256
  117.0 3.4 all-to-all-start.1
  120.8 38.2 %reduce-scatter.2.cloned.1.call-done = bf16[8,512]{1,0:T(8,128)(2,1)} async-done(((bf16[64,512]{1,0:T(8,128)(2,1)}), bf16[8,512]{1,0:T(8,128)(2,1)}) %reduce-scatter.2.cloned.1.call-update) | async-done | bytes 8208 | tf_op jit(solution)/shard_map/reduce_scatter | solution.py:116
  159.0 6.0 %all-reduce.2 = (bf16[8,512]{1,0:T(8,128)(2,1)S(1)}, bf16[8]{0:T(256)(128)(2,1)S(1)}) all-reduce(bf16[8,512]{1,0:T(8,128)(2,1)} %reduce-scatter.2.cloned.1.call-done, bf16[8]{0:T(256)(128)(2,1)S(1)} %dynamic-slice.1), channel_id=1, replica_groups=mesh['group'=4,'dev'=8] {'group'}, use_global_device_ids=true, to_apply=%region_3.4 | all-reduce | flops 4104 | bytes 16416 | tf_op jit(solution)/shard_map/psum | solution.py:112
  166.1 30.5 %all_gather.7 = bf16[64,512]{1,0:T(8,128)(2,1)S(1)} all-gather(bf16[8,512]{1,0:T(8,128)(2,1)S(1)} %fusion.42), channel_id=1, replica_groups=mesh['group'=4,'dev'=8] {'dev'}, dimensions={0}, use_global_device_ids=true | all-gather | bytes 73728 | tf_op jit(solution)/shard_map/all_gather | solution.py:140
  196.6 1.5 fusion.38
  198.1 2.7 multiply_convert_fusion.3
  202.2 2.4 collective-permute-start
  204.6 3.0 collective-permute-start.3
  209.1 1.8 collective-permute-start.5
  210.9 1.5 collective-permute-start.6
  213.3 2.8 collective-permute-done.5
  216.1 1.5 collective-permute-done.6
  217.7 56.7 %while.29 = (s32[]{:T(128)}, f32[512,256]{1,0:T(8,128)}, f32[256,512]{1,0:T(8,128)}, s32[4,1024]{1,0:T(4,128)S(1)}, bf16[320,512]{1,0:T(8,128)(2,1)S(1)}, /*inde...) while((s32[]{:T(128)}, f32[512,256]{1,0:T(8,128)}, ...), condition=%wide.region_8.10_spmd.clone, body=%wide.region_7.9_spmd.clone.sunk | while | flops 810558464 | bytes 11845768 | solution.py:168
  217.7 4.0 gather_fusion.2
  221.7 4.0 gather_fusion.1
  225.7 3.3 convolution_add_fusion.4
  229.0 2.6 convolution_add_fusion.5
  231.7 4.0 gather_fusion.2
  235.7 4.0 gather_fusion.1
  239.7 3.4 convolution_add_fusion.4
  243.1 2.8 convolution_add_fusion.5
  245.9 4.0 gather_fusion.2
  249.9 4.0 gather_fusion.1
  253.9 3.4 convolution_add_fusion.4
  257.4 2.7 convolution_add_fusion.5
  260.1 4.0 gather_fusion.2
  264.1 4.0 gather_fusion.1
  268.1 3.4 convolution_add_fusion.4
  271.6 2.8 convolution_add_fusion.5
  274.4 133.7 %all-reduce.5.cloned.1.call-done = (f32[512,256]{1,0:T(8,128)}, f32[256,512]{1,0:T(8,128)}, f32[512,512]{1,0:T(8,128)}) async-done(((f32[512,256]{1,0:T(8,128)}, f32[256,512]{1,0:T(8,128)}, f32[512,512]{1,0:T(8,128)}), (f32[512,256]{1,0:T(8,128)}, f32[256,512]{1,0:T(8,128)}, f32[512,512]{1,0:T(8,128)})) %all-reduce.5.cloned.1.call-update) | async-done | bytes 2097168 | tf_op jit(solution)/shard_map/psum | solution.py:169
  408.1 1.9 copy.51
  410.0 1.9 copy.52
  411.8 2.3 copy.53
  (127 shorter events, 19.3 us)
Async XLA Ops:
  7.2 157.8 %copy-start = (bf16[512,512]{1,0:T(8,128)(2,1)S(1)}, bf16[512,512]{1,0:T(8,128)(2,1)}, u32[]{:S(2)}) copy-start(bf16[512,512]{1,0:T(8,128)(2,1)} %param.22) | copy-start | bytes 1572868
  10.9 40.7 %all-to-all-start = ((bf16[8,32,512]{2,1,0:T(8,128)(2,1)}), bf16[8,32,512]{2,1,0:T(8,128)(2,1)S(1)}, u32[]{:S(2)}, u32[]{:S(2)}) async-start(bf16[8,32,512]{2,1,0:T(8,128)(2,1)} %bitcast.1), calls=%async_computation | async-start | bytes 524288 | tf_op jit(solution)/shard_map/all_to_all | solution.py:57
  51.7 39.6 %copy-start.6 = (u32[32]{0:T(128)S(1)}, u32[32]{0:T(128)}, u32[]{:S(2)}) copy-start(u32[32]{0:T(128)} %constant.87) | copy-start | bytes 388
  51.7 113.3 %copy-start.2 = (bf16[8,512]{1,0:T(8,128)(2,1)S(1)}, bf16[8,512]{1,0:T(8,128)(2,1)}, u32[]{:S(2)}) copy-start(bf16[8,512]{1,0:T(8,128)(2,1)} %param.19) | copy-start | bytes 24580
  51.7 114.2 %copy-start.3 = (bf16[8,512]{1,0:T(8,128)(2,1)S(1)}, bf16[8,512]{1,0:T(8,128)(2,1)}, u32[]{:S(2)}) copy-start(bf16[8,512]{1,0:T(8,128)(2,1)} %param.29) | copy-start | bytes 24580
  51.7 4.0 copy-start.1
  51.8 5.5 %copy-start.5 = (bf16[256,512]{1,0:T(8,128)(2,1)S(1)}, bf16[256,512]{1,0:T(8,128)(2,1)}, u32[]{:S(2)}) copy-start(bf16[256,512]{1,0:T(8,128)(2,1)} %get-tuple-element.414) | copy-start | bytes 786436 | tf_op jit(solution)/shard_map/while
  59.2 4.0 copy-start.1
  59.3 5.5 %copy-start.5 = (bf16[256,512]{1,0:T(8,128)(2,1)S(1)}, bf16[256,512]{1,0:T(8,128)(2,1)}, u32[]{:S(2)}) copy-start(bf16[256,512]{1,0:T(8,128)(2,1)} %get-tuple-element.414) | copy-start | bytes 786436 | tf_op jit(solution)/shard_map/while
  67.9 4.0 copy-start.1
  67.9 5.5 %copy-start.5 = (bf16[256,512]{1,0:T(8,128)(2,1)S(1)}, bf16[256,512]{1,0:T(8,128)(2,1)}, u32[]{:S(2)}) copy-start(bf16[256,512]{1,0:T(8,128)(2,1)} %get-tuple-element.414) | copy-start | bytes 786436 | tf_op jit(solution)/shard_map/while
  76.5 4.0 copy-start.1
  76.5 5.5 %copy-start.5 = (bf16[256,512]{1,0:T(8,128)(2,1)S(1)}, bf16[256,512]{1,0:T(8,128)(2,1)}, u32[]{:S(2)}) copy-start(bf16[256,512]{1,0:T(8,128)(2,1)} %get-tuple-element.414) | copy-start | bytes 786436 | tf_op jit(solution)/shard_map/while
  85.7 31.2 %all-to-all-start.2 = ((bf16[8,1,32]{2,1,0:T(2,128)(2,1)}), bf16[8,1,32]{2,1,0:T(2,128)(2,1)S(1)}, u32[]{:S(2)}, u32[]{:S(2)}) async-start(bf16[8,1,32]{2,1,0:T(2,128)(2,1)} %convert_element_type.118), calls=%async_computation.2 | async-start | bytes 8192 | tf_op jit(solution)/shard_map/all_to_all | solution.py:98
  91.2 67.8 %reduce-scatter.2.cloned.1.call-start = ((), (), s32[]{:S(2)}) async-start(), calls=%async_computation.4 | async-start | bytes 73728 | tf_op jit(solution)/shard_map/reduce_scatter | solution.py:116
  92.5 105.7 %copy-start.4 = (bf16[512,512]{1,0:T(8,128)(2,1)S(1)}, bf16[512,512]{1,0:T(8,128)(2,1)}, u32[]{:S(2)}) copy-start(bf16[512,512]{1,0:T(8,128)(2,1)} %param.28) | copy-start | bytes 1572868
  117.0 79.6 %all-to-all-start.1 = ((bf16[8,32,512]{2,1,0:T(8,128)(2,1)}), bf16[8,32,512]{2,1,0:T(8,128)(2,1)S(1)}, u32[]{:S(2)}, u32[]{:S(2)}) async-start(bf16[8,32,512]{2,1,0:T(8,128)(2,1)} %bitcast.3), calls=%async_computation.1 | async-start | bytes 524288 | tf_op jit(solution)/shard_map/all_to_all | solution.py:97
  120.4 287.7 %all-reduce.5.cloned.1.call-start = ((), (), s32[]{:S(2)}) async-start(), calls=%async_computation.5 | async-start | bytes 4194304 | tf_op jit(solution)/shard_map/psum | solution.py:169
  202.2 6.9 %collective-permute-start = (bf16[1,32,512]{2,1,0:T(8,128)(2,1)S(1)}, bf16[1,32,512]{2,1,0:T(8,128)(2,1)S(1)}, u32[]{:S(2)}, u32[]{:S(2)}) collective-permute-start(bf16[1,32,512]{2,1,0:T(8,128)(2,1)S(1)} %get-tuple-element.248), channel_id=1, source_target_pairs={{0,7},{1,0},{2,1},{3,2},{4,3},{5,4},{6,5},{7,6},{8,15},{9,8},{10,9... | collective-permute-start | bytes 98312 | tf_op jit(solution)/shard_map/ppermute | solution.py:137
  204.6 6.4 %collective-permute-start.1 = (bf16[1,32,512]{2,1,0:T(8,128)(2,1)S(1)}, bf16[1,32,512]{2,1,0:T(8,128)(2,1)S(1)}, u32[]{:S(2)}, u32[]{:S(2)}) collective-permute-start(bf16[1,32,512]{2,1,0:T(8,128)(2,1)S(1)} %get-tuple-element.247), channel_id=1, source_target_pairs={{0,6},{1,7},{2,0},{3,1},{4,2},{5,3},{6,4},{7,5},{8,14},{9,15},{10,... | collective-permute-start | bytes 98312 | tf_op jit(solution)/shard_map/ppermute | solution.py:137
  204.6 7.8 %collective-permute-start.2 = (bf16[1,32,512]{2,1,0:T(8,128)(2,1)S(1)}, bf16[1,32,512]{2,1,0:T(8,128)(2,1)S(1)}, u32[]{:S(2)}, u32[]{:S(2)}) collective-permute-start(bf16[1,32,512]{2,1,0:T(8,128)(2,1)S(1)} %get-tuple-element.246), channel_id=1, source_target_pairs={{0,5},{1,6},{2,7},{3,0},{4,1},{5,2},{6,3},{7,4},{8,13},{9,14},{10,... | collective-permute-start | bytes 98312 | tf_op jit(solution)/shard_map/ppermute | solution.py:137
  204.6 7.8 %collective-permute-start.3 = (bf16[1,32,512]{2,1,0:T(8,128)(2,1)S(1)}, bf16[1,32,512]{2,1,0:T(8,128)(2,1)S(1)}, u32[]{:S(2)}, u32[]{:S(2)}) collective-permute-start(bf16[1,32,512]{2,1,0:T(8,128)(2,1)S(1)} %get-tuple-element.245), channel_id=1, source_target_pairs={{0,4},{1,5},{2,6},{3,7},{4,0},{5,1},{6,2},{7,3},{8,12},{9,13},{10,... | collective-permute-start | bytes 98312 | tf_op jit(solution)/shard_map/ppermute | solution.py:137
  207.5 5.7 %collective-permute-start.4 = (bf16[1,32,512]{2,1,0:T(8,128)(2,1)S(1)}, bf16[1,32,512]{2,1,0:T(8,128)(2,1)S(1)}, u32[]{:S(2)}, u32[]{:S(2)}) collective-permute-start(bf16[1,32,512]{2,1,0:T(8,128)(2,1)S(1)} %get-tuple-element.244), channel_id=1, source_target_pairs={{0,3},{1,4},{2,5},{3,6},{4,7},{5,0},{6,1},{7,2},{8,11},{9,12},{10,... | collective-permute-start | bytes 98312 | tf_op jit(solution)/shard_map/ppermute | solution.py:137
  209.1 6.9 %collective-permute-start.5 = (bf16[1,32,512]{2,1,0:T(8,128)(2,1)S(1)}, bf16[1,32,512]{2,1,0:T(8,128)(2,1)S(1)}, u32[]{:S(2)}, u32[]{:S(2)}) collective-permute-start(bf16[1,32,512]{2,1,0:T(8,128)(2,1)S(1)} %get-tuple-element.243), channel_id=1, source_target_pairs={{0,2},{1,3},{2,4},{3,5},{4,6},{5,7},{6,0},{7,1},{8,10},{9,11},{10,... | collective-permute-start | bytes 98312 | tf_op jit(solution)/shard_map/ppermute | solution.py:137
  210.9 6.6 %collective-permute-start.6 = (bf16[1,32,512]{2,1,0:T(8,128)(2,1)S(1)}, bf16[1,32,512]{2,1,0:T(8,128)(2,1)S(1)}, u32[]{:S(2)}, u32[]{:S(2)}) collective-permute-start(bf16[1,32,512]{2,1,0:T(8,128)(2,1)S(1)} %get-tuple-element.242), channel_id=1, source_target_pairs={{0,1},{1,2},{2,3},{3,4},{4,5},{5,6},{6,7},{7,0},{8,9},{9,10},{10,1... | collective-permute-start | bytes 98312 | tf_op jit(solution)/shard_map/ppermute | solution.py:137
Sparse Core Ops, SparseCore 0:
  96.0 62.9 reduce-scatter.1
  274.5 133.5 all-reduce.4
